TPU v7x, 32 devices: a whole 2x2x4 slice. The times are simulated.
32 devices in a mesh: slab: 2 (over x), gx: 16 (over z, y, core).
Axes of the slice: x: 2, y: 2, z: 4, core: 2. Of those that a mesh axis runs over, the one named last changes fastest.
Arguments:
- snapshot: float32 [16, 2048, 512], P(None, ('slab', 'gx')), parts along dimension 1, may hold values from -6 to 6
- bitplanes: int32 [32, 8], P(('slab', 'gx')), parts along dimension 0, may hold values from 1 to 15
- slopes: int32 [64], replicated, may hold values from 1 to 536870911, as said below
Outputs:
- coded_values: bfloat16 [16, 2048, 512], P(None, ('slab', 'gx')), parts along dimension 1
- block_distortion: float32 [32, 8], P(('slab', 'gx')), parts along dimension 0
- trial_rates: int32 [12], P('slab'), parts along dimension 0
There are 2 independent parts, one for each index of `slab`. A program takes and returns all parts, laid end to end along the dimension named above; an argument that names none is the same for every part. Nothing has to cross between parts.
Inputs may be any that keep to these rules, and one draw needn't show every extreme that they name: `slopes`: non-decreasing.
All inputs are finite; a program needn't handle non-finite values.
Results may differ from a plain program's by a relative error of at most 0.001.
Values sent between devices are 32-bit elements; how exact they have to be, the bound alone decides.
A program may use at most 64 MiB of HBM per device.

v0:
```python
import jax
import jax.numpy as jnp
from jax import lax
from jax.sharding import PartitionSpec as P

NZ = 16
BX = 64
BY = 64
LEVELS = 3
STEPS = 6
CANDS = 64


ALPHA_LIFT = -1.586134342
BETA_LIFT = -0.05298011854
GAMMA_LIFT = 0.8829110762
DELTA_LIFT = 0.4435068522
KAPPA_SCALE = 1.149604398
QUANT_UNIT = 1.0 / 128.0
LIFT_STEPS = ((ALPHA_LIFT, True), (BETA_LIFT, False), (GAMMA_LIFT, True), (DELTA_LIFT, False))


def padded(array, sides, width):
    for axis, dim in sides:
        size, length = (lax.axis_size(axis), array.shape[dim])
        up = [(i, (i + 1) % size) for i in range(size)]
        down = [(j, i) for i, j in up]
        last = lax.slice_in_dim(array, length - width, length, axis=dim)
        first = lax.slice_in_dim(array, 0, width, axis=dim)
        before = lax.ppermute(last, axis, up)
        after = lax.ppermute(first, axis, down)
        array = jnp.concatenate([before, array, after], axis=dim)
    return array


def odd_rows(values, dim_axis):
    dims = [1, 1, 1]
    dims[dim_axis] = values.shape[dim_axis]
    return lax.broadcasted_iota(jnp.int32, tuple(dims), dim_axis) % 2 == 1


def periodic_sides(values, dim_axis):
    return (jnp.roll(values, 1, dim_axis), jnp.roll(values, -1, dim_axis))


def mirror_sides(values, dim_axis):
    length = values.shape[dim_axis]
    behind = jnp.concatenate(
        [
            lax.slice_in_dim(values, 1, 2, axis=dim_axis),
            lax.slice_in_dim(values, 0, length - 1, axis=dim_axis),
        ],
        dim_axis,
    )
    forward = jnp.concatenate(
        [
            lax.slice_in_dim(values, 1, length, axis=dim_axis),
            lax.slice_in_dim(values, length - 2, length - 1, axis=dim_axis),
        ],
        dim_axis,
    )
    return (behind, forward)


def lift_axis(values, dim_axis, sides):
    odd_mask = odd_rows(values, dim_axis)
    for coefficient, on_odd in LIFT_STEPS:
        behind, forward = sides(values, dim_axis)
        target = odd_mask if on_odd else jnp.logical_not(odd_mask)
        values = values + jnp.where(target, coefficient * (behind + forward), 0.0)
    return values * jnp.where(odd_mask, 1.0 / KAPPA_SCALE, KAPPA_SCALE)


def plane_table():
    plane_ids = jnp.arange(1, 16, dtype=jnp.int32)
    return (plane_ids, jnp.left_shift(jnp.int32(1), 2 * plane_ids))


def kept_planes(bitplanes, trial_slope):
    plane_ids, powers = plane_table()
    hits = (plane_ids[None, None, :] <= bitplanes[:, :, None]) & (
        powers[None, None, :] >= trial_slope
    )
    return jnp.sum(hits.astype(jnp.int32), axis=2, dtype=jnp.int32)


def pick_entry(table, index):
    positions = jnp.arange(table.shape[0], dtype=jnp.int32)
    return jnp.sum(jnp.where(positions == index, table, 0), dtype=jnp.int32)


def body(snapshot, bitplanes, slopes):
    coeffs = snapshot
    for tier_index in range(LEVELS):
        stride = 2**tier_index
        subgrid = coeffs[::stride, ::stride, ::stride]
        extended = padded(subgrid, (("gx", 1),), 4)
        extended = lift_axis(extended, 1, periodic_sides)
        subgrid = extended[:, 4:-4, :]
        subgrid = lift_axis(subgrid, 2, periodic_sides)
        subgrid = lift_axis(subgrid, 0, mirror_sides)
        coeffs = coeffs.at[::stride, ::stride, ::stride].set(subgrid)
    target_rate = 2 * bitplanes.shape[0] * lax.axis_size("gx") * bitplanes.shape[1]
    lower = jnp.int32(0)
    upper_end = jnp.int32(CANDS - 1)
    trial_list = []
    for step_index in range(STEPS):
        middle = (lower + upper_end) // 2
        local_rate = jnp.sum(kept_planes(bitplanes, pick_entry(slopes, middle)), dtype=jnp.int32)
        rate_sum = lax.psum(local_rate, "gx")
        trial_list.append(rate_sum)
        accept = rate_sum <= target_rate
        upper_end = jnp.where(accept, middle, upper_end)
        lower = jnp.where(accept, lower, middle + 1)
    kept_final = kept_planes(bitplanes, pick_entry(slopes, lower))
    step_size = QUANT_UNIT * jnp.left_shift(jnp.int32(1), bitplanes - kept_final).astype(
        jnp.float32
    )
    step_map = jnp.repeat(jnp.repeat(step_size, BX, axis=0), BY, axis=1)
    magnitude = jnp.abs(coeffs)
    coded_values = (jnp.sign(coeffs) * jnp.maximum(magnitude - step_map, 0.0)).astype(jnp.bfloat16)
    squared_step = step_map * step_map
    ratios = jnp.minimum(coeffs * coeffs, squared_step) / squared_step
    plane_sum = jnp.sum(ratios, axis=0)
    blocks = plane_sum.reshape(bitplanes.shape[0], BX, bitplanes.shape[1], BY).sum(axis=(1, 3)) / (
        NZ * BX * BY
    )
    return (coded_values, blocks, jnp.stack(trial_list))


def solution(mesh):
    return jax.shard_map(
        body,
        mesh=mesh,
        in_specs=(P(None, ("slab", "gx"), None), P(("slab", "gx"), None), P()),
        out_specs=(P(None, ("slab", "gx"), None), P(("slab", "gx"), None), P("slab")),
        check_vma=False,
    )
```

profile of v0, /device:TPU:0, one launch (start us, length us, event | category | flops | bytes accessed | tf_op | source)
XLA Modules:
  0.0 438.4 jit_solution(14832641071903336317)
XLA Ops:
  0.7 1.1 fusion.183
  1.8 5.5 %collective-permute-start.1 = (f32[16,4,512]{2,1,0:T(4,128)S(1)}, f32[16,4,512]{2,1,0:T(4,128)S(1)}, u32[]{:S(2)}, u32[]{:S(2)}) collective-permute-start(f32[16,4,512]{2,1,0:T(4,128)S(1)} %get-tuple-element.73), channel_id=1, source_target_pairs={{1,0},{2,1},{3,2},{4,3},{5,4},{6,5},{7,6},{8,7},{9,8},{10,9},{11,1... | collective-permute-start | bytes 393224 | tf_op jit(solution)/shard_map/ppermute | solution.py:31
  7.8 0.9 fusion.44
  13.0 0.7 convert_reduce_fusion.6
  14.3 12.7 %psum.42 = s32[]{:T(128)} all-reduce(s32[]{:T(128)} %convert_reduce_fusion.6), channel_id=1, replica_groups=mesh['slab'=2,'gx'=16] {'gx'}, use_global_device_ids=true, to_apply=%region_4.5 | all-reduce | flops 1 | bytes 8 | tf_op jit(solution)/shard_map/psum | solution.py:110
  28.9 0.7 convert_reduce_fusion.5
  29.6 8.8 %psum.43 = s32[]{:T(128)} all-reduce(s32[]{:T(128)} %convert_reduce_fusion.5), channel_id=1, replica_groups=mesh['slab'=2,'gx'=16] {'gx'}, use_global_device_ids=true, to_apply=%region_7.8 | all-reduce | flops 1 | bytes 8 | tf_op jit(solution)/shard_map/psum | solution.py:110
  40.3 0.7 convert_reduce_fusion.4
  41.0 12.7 %psum.44 = s32[]{:T(128)} all-reduce(s32[]{:T(128)} %convert_reduce_fusion.4), channel_id=1, replica_groups=mesh['slab'=2,'gx'=16] {'gx'}, use_global_device_ids=true, to_apply=%region_10.11 | all-reduce | flops 1 | bytes 8 | tf_op jit(solution)/shard_map/psum | solution.py:110
  55.7 0.7 convert_reduce_fusion.3
  56.4 8.8 %psum.45 = s32[]{:T(128)} all-reduce(s32[]{:T(128)} %convert_reduce_fusion.3), channel_id=1, replica_groups=mesh['slab'=2,'gx'=16] {'gx'}, use_global_device_ids=true, to_apply=%region_13.14 | all-reduce | flops 1 | bytes 8 | tf_op jit(solution)/shard_map/psum | solution.py:110
  67.1 0.7 convert_reduce_fusion.2
  67.8 12.8 %psum.46 = s32[]{:T(128)} all-reduce(s32[]{:T(128)} %convert_reduce_fusion.2), channel_id=1, replica_groups=mesh['slab'=2,'gx'=16] {'gx'}, use_global_device_ids=true, to_apply=%region_16.17 | all-reduce | flops 1 | bytes 8 | tf_op jit(solution)/shard_map/psum | solution.py:110
  82.6 0.7 convert_reduce_fusion.1
  83.3 8.8 %psum.47 = s32[]{:T(128)} all-reduce(s32[]{:T(128)} %convert_reduce_fusion.1), channel_id=1, replica_groups=mesh['slab'=2,'gx'=16] {'gx'}, use_global_device_ids=true, to_apply=%region_19.20 | all-reduce | flops 1 | bytes 8 | tf_op jit(solution)/shard_map/psum | solution.py:110
  96.9 1.0 fusion.2
  98.6 0.9 fusion.5
  100.1 0.9 fusion.8
  101.7 1.0 fusion.12
  102.7 1.0 fusion.160
  103.9 1.0 slice_add_fusion
  104.9 0.8 fusion.181
  105.9 1.0 fusion.17
  106.8 0.8 fusion.179
  107.8 1.2 fusion.20
  109.0 0.8 fusion.177
  109.9 1.0 fusion.24
  111.6 0.8 fusion.27
  113.0 0.9 fusion.30
  114.5 0.9 fusion.33
  116.0 0.9 fusion.37
  116.9 9.3 %slice.577 = f32[8,32,256]{2,1,0:T(8,128)S(1)} slice(f32[16,64,512]{2,1,0:T(8,128)S(1)} %fusion.37), slice={[0:16:2], [0:64:2], [0:512:2]} | slice | bytes 524288 | tf_op jit(solution)/shard_map/slice | solution.py:96
  126.3 1.4 collective-permute-start.3
  128.5 2.1 copy.6
  130.6 3.2 collective-permute-done.2
  137.2 240.5 %scatter_fusion = f32[524288]{0:T(1024)S(1)} fusion(f32[524288]{0:T(1024)S(1)} %bitcast.29, s32[65536]{0:T(1024)S(1)} %bitcast.31, f32[65536]{0:T(1024)S(1)} %bitcast.32), kind=kCustom, calls=%fused_computation | custom fusion | bytes 1048576
  377.7 1.5 reshape.844
  379.3 3.2 slice.629
  382.5 1.4 collective-permute-start.5
  384.0 4.3 stack.27
  388.3 1.3 collective-permute-done.4
  391.5 31.2 %scatter_fusion.1 = f32[524288]{0:T(1024)S(1)} fusion(f32[524288]{0:T(1024)S(1)} %scatter_fusion, s32[8192]{0:T(1024)S(1)} %bitcast.35, f32[8192]{0:T(1024)S(1)} %bitcast.36), kind=kCustom, calls=%fused_computation.1 | custom fusion | bytes 131072
  422.8 2.8 fusion.159
  425.5 1.7 reshape.849
  427.3 2.7 reshape.850
  430.0 2.7 reshape.851
  432.7 1.9 fusion.38
  435.3 3.1 multiply_convert_fusion
  (208 shorter events, 27.6 us)
Async XLA Ops:
  0.6 8.3 %copy-start.10 = (s32[3]{0:T(128)S(1)}, s32[3]{0:T(128)}, u32[]{:S(2)}) copy-start(s32[3]{0:T(128)} %constant.251) | copy-start | bytes 40
  0.6 8.0 %copy-start.11 = (s32[3]{0:T(128)S(1)}, s32[3]{0:T(128)}, u32[]{:S(2)}) copy-start(s32[3]{0:T(128)} %constant.248) | copy-start | bytes 40
  0.7 11.1 %copy-start.15 = (s32[64]{0:T(128)S(1)}, s32[64]{0:T(128)}, u32[]{:S(2)}) copy-start(s32[64]{0:T(128)} %param.9) | copy-start | bytes 772
  0.7 12.4 %copy-start.3 = (s32[1,8]{1,0:T(1,128)S(1)}, s32[1,8]{1,0:T(1,128)}, u32[]{:S(2)}) copy-start(s32[1,8]{1,0:T(1,128)} %param.8) | copy-start | bytes 100
  1.8 94.1 %copy-start = (f32[16,64,512]{2,1,0:T(8,128)S(1)}, f32[16,64,512]{2,1,0:T(8,128)}, u32[]{:S(2)}) copy-start(f32[16,64,512]{2,1,0:T(8,128)} %param.7) | copy-start | bytes 6291460
  1.8 94.1 %collective-permute-start.1 = (f32[16,4,512]{2,1,0:T(4,128)S(1)}, f32[16,4,512]{2,1,0:T(4,128)S(1)}, u32[]{:S(2)}, u32[]{:S(2)}) collective-permute-start(f32[16,4,512]{2,1,0:T(4,128)S(1)} %get-tuple-element.73), channel_id=1, source_target_pairs={{1,0},{2,1},{3,2},{4,3},{5,4},{6,5},{7,6},{8,7},{9,8},{10,9},{11,1... | collective-permute-start | bytes 393224 | tf_op jit(solution)/shard_map/ppermute | solution.py:31
  7.3 88.6 %collective-permute-start = (f32[16,4,512]{2,1,0:T(4,128)S(1)}, f32[16,4,512]{2,1,0:T(4,128)S(1)}, u32[]{:S(2)}, u32[]{:S(2)}) collective-permute-start(f32[16,4,512]{2,1,0:T(4,128)S(1)} %get-tuple-element.72), channel_id=1, source_target_pairs={{0,1},{1,2},{2,3},{3,4},{4,5},{5,6},{6,7},{7,8},{8,9},{9,10},{10,1... | collective-permute-start | bytes 393224 | tf_op jit(solution)/shard_map/ppermute | solution.py:30
  116.9 11.5 %copy-start.1 = (f32[16,64,512]{2,1,0:T(8,128)}, f32[16,64,512]{2,1,0:T(8,128)S(1)}, u32[]{:S(2)}) copy-start(f32[16,64,512]{2,1,0:T(8,128)S(1)} %fusion.37) | copy-start | bytes 6291460
  126.3 4.3 collective-permute-start.3
  127.7 6.0 %collective-permute-start.2 = (f32[8,4,256]{2,1,0:T(4,128)S(1)}, f32[8,4,256]{2,1,0:T(4,128)S(1)}, u32[]{:S(2)}, u32[]{:S(2)}) collective-permute-start(f32[8,4,256]{2,1,0:T(4,128)S(1)} %get-tuple-element.120), channel_id=1, source_target_pairs={{0,1},{1,2},{2,3},{3,4},{4,5},{5,6},{6,7},{7,8},{8,9},{9,10},{10,1... | collective-permute-start | bytes 98312 | tf_op jit(solution)/shard_map/ppermute | solution.py:30
  377.7 6.1 %copy-start.14 = (f32[8]{0:T(128)S(1)}, f32[8]{0:T(128)}, u32[]{:S(2)}) copy-start(f32[8]{0:T(128)} %fusion.149) | copy-start | bytes 100
  377.7 11.9 %copy-start.7 = (pred[24]{0:T(512)(128)(4,1)S(1)}, pred[24]{0:T(512)(128)(4,1)}, u32[]{:S(2)}) copy-start(pred[24]{0:T(512)(128)(4,1)} %fusion.136) | copy-start | bytes 76
  377.7 12.1 %copy-start.6 = (pred[24]{0:T(512)(128)(4,1)S(1)}, pred[24]{0:T(512)(128)(4,1)}, u32[]{:S(2)}) copy-start(pred[24]{0:T(512)(128)(4,1)} %fusion.152) | copy-start | bytes 76
  377.7 12.3 %copy-start.13 = (f32[24]{0:T(128)S(1)}, f32[24]{0:T(128)}, u32[]{:S(2)}) copy-start(f32[24]{0:T(128)} %broadcast_select_fusion.6) | copy-start | bytes 292
  379.2 11.0 %copy-start.5 = (pred[128]{0:T(512)(128)(4,1)S(1)}, pred[128]{0:T(512)(128)(4,1)}, u32[]{:S(2)}) copy-start(pred[128]{0:T(512)(128)(4,1)} %fusion.137) | copy-start | bytes 388
  379.2 11.2 %copy-start.4 = (pred[128]{0:T(512)(128)(4,1)S(1)}, pred[128]{0:T(512)(128)(4,1)}, u32[]{:S(2)}) copy-start(pred[128]{0:T(512)(128)(4,1)} %fusion.151) | copy-start | bytes 388
  379.2 11.8 %copy-start.12 = (f32[128]{0:T(128)S(1)}, f32[128]{0:T(128)}, u32[]{:S(2)}) copy-start(f32[128]{0:T(128)} %broadcast_select_fusion.5) | copy-start | bytes 1540
  379.2 11.9 %copy-start.8 = (pred[4]{0:T(512)(128)(4,1)S(1)}, pred[4]{0:T(512)(128)(4,1)}, u32[]{:S(2)}) copy-start(pred[4]{0:T(512)(128)(4,1)} %fusion.138) | copy-start | bytes 16
  379.2 12.0 %copy-start.9 = (pred[4]{0:T(512)(128)(4,1)S(1)}, pred[4]{0:T(512)(128)(4,1)}, u32[]{:S(2)}) copy-start(pred[4]{0:T(512)(128)(4,1)} %fusion.150) | copy-start | bytes 16
  382.5 5.9 %collective-permute-start.5 = (f32[4,4,128]{2,1,0:T(4,128)S(1)}, f32[4,4,128]{2,1,0:T(4,128)S(1)}, u32[]{:S(2)}, u32[]{:S(2)}) collective-permute-start(f32[4,4,128]{2,1,0:T(4,128)S(1)} %get-tuple-element.169), channel_id=1, source_target_pairs={{1,0},{2,1},{3,2},{4,3},{5,4},{6,5},{7,6},{8,7},{9,8},{10,9},{11,1... | collective-permute-start | bytes 24584 | tf_op jit(solution)/shard_map/ppermute | solution.py:31
  383.8 5.8 %collective-permute-start.4 = (f32[4,4,128]{2,1,0:T(4,128)S(1)}, f32[4,4,128]{2,1,0:T(4,128)S(1)}, u32[]{:S(2)}, u32[]{:S(2)}) collective-permute-start(f32[4,4,128]{2,1,0:T(4,128)S(1)} %get-tuple-element.168), channel_id=1, source_target_pairs={{0,1},{1,2},{2,3},{3,4},{4,5},{5,6},{6,7},{7,8},{8,9},{9,10},{10,1... | collective-permute-start | bytes 24584 | tf_op jit(solution)/shard_map/ppermute | solution.py:30
  389.7 1.8 copy-start.2
where the time goes:
time: 439 us; the launch traced here: 438 us
  local copies, waits for them, and re-layouts  313 us (71%)
  blocking collectives  64.5 us (15%)
  other arithmetic  43 us (10%)
  starting transfers between devices  8.28 us (2%)
  between operations  5.7 us (1%)
  waiting for transfers between devices  4.41 us (1%)
    unnamed x37, local copies, waits for them, and re-layouts  274 us
    psum x6, blocking collectives, body(): rate_sum = lax.psum(local_rate, 'gx')  64.5 us
    slice x2, local copies, waits for them, and re-layouts, body(): subgrid = coeffs[::stride, ::stride, ::stride]  12.5 us
    add x27, other arithmetic, lift_axis(): values = values + jnp.where(target, coefficient * (behind + forward), 0.0)  10.5 us
  transfers between devices with their start and end apart: 6, of which 2 were waited for; matrix products, arithmetic and copies ran while one was open for 6% of the time, Pallas kernels for 0%

commit v1 on v0

v1 whole, which is shorter than its diff:
```python
import functools

import jax
import jax.numpy as jnp
from jax import lax
from jax.experimental import pallas as pl
from jax.experimental.pallas import tpu as pltpu
from jax.sharding import PartitionSpec as P

NZ, NXL, NY = 16, 64, 512
LANES = 128
NJ = NY // LANES
ROWS = NZ * NXL
CANDS = 64
STEPS = 6
GROUPS = 4

AL = -1.586134342
BE = -0.05298011854
GA = 0.8829110762
DE = 0.4435068522
KA = 1.149604398
QUANT_UNIT = 1.0 / 128.0
MESH = pl.DeviceIdType.MESH


def lane_iota(rows=1):
    return lax.broadcasted_iota(jnp.int32, (rows, LANES), 1)


def y_lift(vals, level):
    s = 2**level
    lane = lane_iota()
    on_even = lane % (2 * s) == 0
    on_odd = lane % (2 * s) == s
    low = lane < s
    high = lane >= LANES - s
    for coefficient, odd in ((AL, True), (BE, False), (GA, True), (DE, False)):
        back = [pltpu.roll(v, s, 1) for v in vals]
        forth = [pltpu.roll(v, LANES - s, 1) for v in vals]
        if odd:
            forth = [jnp.where(high, forth[(j + 1) % NJ], forth[j]) for j in range(NJ)]
        else:
            back = [jnp.where(low, back[(j - 1) % NJ], back[j]) for j in range(NJ)]
        weight = jnp.where(on_odd if odd else on_even, coefficient, 0.0)
        vals = [vals[j] + weight * (back[j] + forth[j]) for j in range(NJ)]
    return vals


def y_scale(level):
    s = 2**level
    lane = lane_iota()
    scale = jnp.where(lane % (2 * s) == 0, KA, 1.0 / KA)
    return jnp.where(lane % s == 0, scale, 1.0), lane % s == 0


def weights(level):
    if level == 0:
        return AL, BE, GA, DE
    own = lane_iota() % 2**level == 0
    return tuple(jnp.where(own, c, 0.0) for c in (AL, BE, GA, DE))


def z_lift(v, level):
    n = len(v)
    w = weights(level)
    v = list(v)
    for coefficient, first in ((w[0], 1), (w[1], 0), (w[2], 1), (w[3], 0)):
        for k in range(first, n, 2):
            a = v[k - 1] if k > 0 else v[k + 1]
            b = v[k + 1] if k < n - 1 else v[k - 1]
            v[k] = v[k] + coefficient * (a + b)
    return v


def shift_up(v, last):
    rows = v.shape[0]
    index = lax.broadcasted_iota(jnp.int32, v.shape, 0)
    return jnp.where(index == rows - 1, last, pltpu.roll(v, rows - 1, 0))


def shift_down(v, first):
    index = lax.broadcasted_iota(jnp.int32, v.shape, 0)
    return jnp.where(index == 0, first, pltpu.roll(v, 1, 0))


def x_lift(even, odd, p, r, e, t, level):
    rows = even.shape[0]
    al, be, ga, de = weights(level)
    d1 = odd + al * (even + shift_up(even, e))
    d1_before = p + al * even[0:1]
    s1 = even + be * (d1 + shift_down(d1, d1_before))
    s1_before = r + be * d1_before
    s1_after = t + be * d1[rows - 1 : rows]
    d2 = d1 + ga * (s1 + shift_up(s1, s1_after))
    d2_before = d1_before + ga * (s1_before + s1[0:1])
    s2 = s1 + de * (d2 + shift_down(d2, d2_before))
    return s2, d2


def kernel(
    n, x_hbm, bits, slopes, coded, dist, trial,
    c0, c1, c2, ob, slope_row, rates,
    sr0, sl0, fl0, fr0, sr1, sl1, fl1, fr1, sr2, sl2, fl2, fr2,
    in_sem, out_sem, rate_send, rate_recv, edge_send, edge_recv,
):
    me = lax.axis_index("gx")
    right, left = lax.rem(me + 1, n), lax.rem(me + n - 1, n)

    group_rows = ROWS // GROUPS
    loads = []
    for g in range(GROUPS):
        for j in range(NJ):
            copy = pltpu.make_async_copy(
                x_hbm.at[pl.ds(g * group_rows, group_rows), pl.ds(j * LANES, LANES)],
                c0.at[j, pl.ds(g * group_rows, group_rows)],
                in_sem.at[g, j],
            )
            copy.start()
            loads.append(copy)

    barrier = pltpu.get_barrier_semaphore()

    def greet(k, carry):
        pl.semaphore_signal(
            barrier, inc=1, device_id={"gx": lax.rem(me + k, n)}, device_id_type=MESH
        )
        return carry

    lax.fori_loop(1, n, greet, 0)

    slope_row[...] = jnp.full((1, LANES), 536870911, jnp.int32)
    slope_row[:, 0:CANDS] = slopes[...]
    trial_slopes = slope_row[...]
    skipped = jnp.zeros((1, LANES), jnp.int32)
    for q in range(1, 16):
        skipped = skipped + jnp.where(trial_slopes > 4**q, 1, 0)
    own = jnp.zeros((1, LANES), jnp.int32)
    for b in range(8):
        own = own + jnp.maximum(bits[0, b] - skipped, 0)
    rates[me] = own

    pl.semaphore_wait(barrier, n - 1)

    def rate_copy(k, row):
        return pltpu.make_async_remote_copy(
            src_ref=rates.at[row],
            dst_ref=rates.at[row],
            send_sem=rate_send.at[k],
            recv_sem=rate_recv.at[k],
            device_id={"gx": lax.rem(me + k, n)},
            device_id_type=MESH,
        )

    def send_rate(k, carry):
        rate_copy(k, me).start()
        return carry

    lax.fori_loop(1, n, send_rate, 0)

    chunk = 32
    levels = (
        (c0, NZ, NXL, sr0, sl0, fl0, fr0),
        (c1, NZ // 2, NXL // 2, sr1, sl1, fl1, fr1),
        (c2, NZ // 4, NXL // 4, sr2, sl2, fl2, fr2),
    )
    for level, (buf, nz, nx, send_right, send_left, from_left, from_right) in enumerate(levels):
        rows = nz * nx

        def y_body(i, carry, buf=buf, level=level):
            at = pl.ds(pl.multiple_of(i * chunk, chunk), chunk)
            vals = y_lift([buf[j, at, :] for j in range(NJ)], level)
            for j in range(NJ):
                buf[j, at, :] = vals[j]
            return carry

        if level == 0:
            for g in range(GROUPS):
                for j in range(NJ):
                    loads[g * NJ + j].wait()
                per = group_rows // chunk
                lax.fori_loop(g * per, (g + 1) * per, y_body, 0)
        else:
            lax.fori_loop(0, rows // chunk, y_body, 0)

        def z_body(i, carry, buf=buf, nz=nz, nx=nx, level=level):
            at = [pl.ds(pl.multiple_of(k * nx + i * 8, 8), 8) for k in range(nz)]
            for j in range(NJ):
                planes = z_lift([buf[j, at[k], :] for k in range(nz)], level)
                for k in range(nz):
                    buf[j, at[k], :] = planes[k]
            return carry

        lax.fori_loop(0, nx // 8, z_body, 0)

        for j in range(NJ):
            def row(x):
                return buf[j, pl.ds(x, nz, stride=nx), :]

            a, b, c, d = row(nx - 4), row(nx - 3), row(nx - 2), row(nx - 1)
            send_right[0, j] = d + AL * c
            send_right[1, j] = c + BE * (b + AL * (a + c))
            a, b, c = row(0), row(1), row(2)
            send_left[0, j] = a
            send_left[1, j] = a + BE * (b + AL * (a + c))
        copies = []
        for side, src, dst, to in (
            (0, send_right, from_left, right),
            (1, send_left, from_right, left),
        ):
            copy = pltpu.make_async_remote_copy(
                src_ref=src,
                dst_ref=dst,
                send_sem=edge_send.at[level, side],
                recv_sem=edge_recv.at[level, side],
                device_id={"gx": to},
                device_id_type=MESH,
            )
            copy.start()
            copies.append(copy)
        for copy in copies:
            copy.wait()

        lanes_scale, lanes_own = y_scale(level)

        def x_body(i, carry, level=level, buf=buf, nz=nz, nx=nx,
                   from_left=from_left, from_right=from_right,
                   lanes_scale=lanes_scale, lanes_own=lanes_own):
            half = nx // 2
            step = 2**level
            for parity in range(2):
                k = 2 * i + parity
                z_gain = 1.0 / KA if parity else KA
                even_scale = jnp.where(lanes_own, lanes_scale * (z_gain * KA), 1.0)
                odd_scale = jnp.where(lanes_own, lanes_scale * (z_gain / KA), 1.0)
                base = k * step * NXL
                for j in range(NJ):
                    even = buf[j, pl.ds(k * nx, half, stride=2), :]
                    odd = buf[j, pl.ds(k * nx + 1, half, stride=2), :]
                    at = pl.ds(k, 1)
                    s2, d2 = x_lift(
                        even, odd, from_left[0, j, at, :], from_left[1, j, at, :],
                        from_right[0, j, at, :], from_right[1, j, at, :], level,
                    )
                    s2 = s2 * even_scale
                    d2 = d2 * odd_scale
                    c0[j, pl.ds(base + step, half, stride=2 * step), :] = d2
                    if parity == 0 and level < 2:
                        to = pl.ds(pl.multiple_of(i * half, 8), half)
                        levels[level + 1][0][j, to, :] = s2
                    else:
                        c0[j, pl.ds(base, half, stride=2 * step), :] = s2
            return carry

        lax.fori_loop(0, nz // 2, x_body, 0)

    def take_rate(k, carry):
        rate_copy(k, lax.rem(me - k + n, n)).wait_recv()
        return carry

    lax.fori_loop(1, n, take_rate, 0)
    total = jnp.sum(rates[...], axis=0)
    lane = lane_iota()
    target = 2 * 8 * n
    total_f = total.astype(jnp.float32)
    over = jnp.where((lane < CANDS - 1) & (total > target), 1.0, 0.0)
    lower = jnp.sum(over).astype(jnp.int32)
    for step in range(STEPS):
        span = 2 ** (STEPS - step)
        middle = (lower // span) * span + span // 2 - 1
        trial[step] = jnp.sum(jnp.where(lane == middle, total_f, 0.0)).astype(jnp.int32)
    skip = jnp.sum(jnp.where(lane == lower, skipped.astype(jnp.float32), 0.0)).astype(jnp.int32)

    step_sizes, squares = [], []
    for j in range(NJ):
        planes = jnp.where(
            lane < 64, jnp.minimum(bits[0, 2 * j], skip), jnp.minimum(bits[0, 2 * j + 1], skip)
        )
        step_sizes.append(QUANT_UNIT * jnp.left_shift(jnp.int32(1), planes).astype(jnp.float32))
        squares.append(jnp.zeros((8, LANES), jnp.float32))

    per = group_rows // chunk
    stores = []
    for g in range(GROUPS):
        def code_body(i, sums):
            at = pl.ds(pl.multiple_of(i * chunk, chunk), chunk)
            out = []
            for j in range(NJ):
                values = c0[j, at, :]
                inside = jnp.clip(values, -step_sizes[j], step_sizes[j])
                ob[at, pl.ds(j * LANES, LANES)] = (values - inside).astype(jnp.bfloat16)
                part = inside * inside
                acc = sums[j]
                for m in range(chunk // 8):
                    acc = acc + part[8 * m : 8 * m + 8]
                out.append(acc)
            return tuple(out)

        squares = lax.fori_loop(g * per, (g + 1) * per, code_body, tuple(squares))
        at = pl.ds(g * group_rows, group_rows)
        copy = pltpu.make_async_copy(ob.at[at], coded.at[at], out_sem.at[g])
        copy.start()
        stores.append(copy)

    result = jnp.zeros((1, 8), jnp.float32)
    column = lax.broadcasted_iota(jnp.int32, (1, 8), 1)
    for j in range(NJ):
        ratio = jnp.sum(squares[j], axis=0, keepdims=True) / (step_sizes[j] * step_sizes[j])
        for half in range(2):
            mine = (lane >= 64) if half else (lane < 64)
            mean = jnp.sum(jnp.where(mine, ratio, 0.0), axis=1, keepdims=True) / (NZ * 64 * 64)
            result = jnp.where(column == 2 * j + half, mean, result)
    dist[...] = result

    def end_rate(k, carry):
        rate_copy(k, me).wait_send()
        return carry

    lax.fori_loop(1, n, end_rate, 0)
    for copy in stores:
        copy.wait()


def body(snapshot, bitplanes, slopes):
    n = lax.axis_size("gx")
    vmem = pl.BlockSpec(memory_space=pltpu.VMEM)
    smem = pl.BlockSpec(memory_space=pltpu.SMEM)
    hbm = pl.BlockSpec(memory_space=pl.ANY)
    edges = []
    for level in range(3):
        edges += [pltpu.VMEM((2, NJ, NZ >> level, LANES), jnp.float32)] * 4
    coded, dist, trial = pl.pallas_call(
        functools.partial(kernel, n),
        out_shape=(
            jax.ShapeDtypeStruct((ROWS, NY), jnp.bfloat16),
            jax.ShapeDtypeStruct((1, 8), jnp.float32),
            jax.ShapeDtypeStruct((STEPS,), jnp.int32),
        ),
        in_specs=[hbm, smem, vmem],
        out_specs=(hbm, vmem, smem),
        scratch_shapes=[
            pltpu.VMEM((NJ, ROWS, LANES), jnp.float32),
            pltpu.VMEM((NJ, ROWS // 4, LANES), jnp.float32),
            pltpu.VMEM((NJ, ROWS // 16, LANES), jnp.float32),
            pltpu.VMEM((ROWS, NY), jnp.bfloat16),
            pltpu.VMEM((1, LANES), jnp.int32),
            pltpu.VMEM((n, 1, LANES), jnp.int32),
            *edges,
            pltpu.SemaphoreType.DMA((GROUPS, NJ)),
            pltpu.SemaphoreType.DMA((GROUPS,)),
            pltpu.SemaphoreType.DMA((n,)),
            pltpu.SemaphoreType.DMA((n,)),
            pltpu.SemaphoreType.DMA((3, 2)),
            pltpu.SemaphoreType.DMA((3, 2)),
        ],
        compiler_params=pltpu.CompilerParams(
            collective_id=0, has_side_effects=True, vmem_limit_bytes=32 * 1024 * 1024
        ),
    )(snapshot.reshape(ROWS, NY), bitplanes, slopes.reshape(1, CANDS))
    return coded.reshape(NZ, NXL, NY), dist, trial


def solution(mesh):
    return jax.shard_map(
        body,
        mesh=mesh,
        in_specs=(P(None, ("slab", "gx"), None), P(("slab", "gx"), None), P()),
        out_specs=(P(None, ("slab", "gx"), None), P(("slab", "gx"), None), P("slab")),
        check_vma=False,
    )
```

time: 439 us -> 42.4 us (0.10)
  local copies, waits for them, and re-layouts: 313 us -> 4.89 us
  blocking collectives: 64.5 us -> 0 us
  other arithmetic: 43 us -> 0 us
  Pallas kernels: 0 us -> 36.7 us
  starting transfers between devices: 8.28 us -> 0 us
  between operations: 5.7 us -> 0.65 us
  waiting for transfers between devices: 4.41 us -> 0 us
    unnamed x37 -> x9, local copies, waits for them, and re-layouts: 274 us -> 4.89 us
    psum x6 -> x0, blocking collectives: 64.5 us -> none  [body(): rate_sum = lax.psum(local_rate, 'gx')]
    pallas_call x0 -> x1, Pallas kernels: none -> 36.7 us  [body(): pl.pallas_call(functools.partial(kernel, n), out_shape=(jax.ShapeDtypeStr...]
    slice x80 -> x0, local copies, waits for them, and re-layouts: 24.7 us -> none  [the longest x2 12.5 us: body(): subgrid = coeffs[::stride, ::stride, ::stride]]
    reduce_sum x16 -> x0, other arithmetic: 10.8 us -> none  [the longest x7 4.42 us: pick_entry(): return jnp.sum(jnp.where(positions == index, table, 0), dtype=jnp.int32)]
    add x28 -> x0, other arithmetic: 10.5 us -> none  [the longest x27 10.5 us: lift_axis(): values = values + jnp.where(target, coefficient * (behind + forward), 0.0)]
    ppermute x6 -> x0, starting transfers between devices: 8.28 us -> none  [the longest x3 8.27 us: padded(): after = lax.ppermute(first, axis, down)]
    ge x7 -> x0, other arithmetic: 4.56 us -> none  [kept_planes(): powers[None, None, :] >= trial_slope]
  transfers between devices with their start and end apart: 6 -> 0, of which waited for: 2 -> 0; matrix products, arithmetic and copies ran while one was open for 6% -> 0% of each run, Pallas kernels for 0% -> 0%
where the time goes in v1:
time: 42.4 us; the launch traced here: 42.3 us
  Pallas kernels  36.7 us (87%)
  local copies, waits for them, and re-layouts  4.89 us (12%)
  between operations  0.65 us (2%)
    pallas_call x1, Pallas kernels, body(): pl.pallas_call(functools.partial(kernel, n), out_shape=(jax.ShapeDtypeStr...  36.7 us
    unnamed x9, local copies, waits for them, and re-layouts  4.89 us

profile of v1, /device:TPU:0, one launch (start us, length us, event | category | flops | bytes accessed | tf_op | source)
XLA Modules:
  0.0 42.3 jit_solution(397845147857596635)
XLA Ops:
  0.6 0.0 copy-start
  0.6 1.6 %copy-done = f32[16,64,512]{2,1,0:T(8,128)S(1)} copy-done((f32[16,64,512]{2,1,0:T(8,128)S(1)}, f32[16,64,512]{2,1,0:T(8,128)}, u32[]{:S(2)}) %copy-start) | copy-done | bytes 2097176
  2.2 0.0 copy-start.1
  2.2 0.7 %copy-done.1 = s32[1,8]{1,0:T(1,128)S(1)} copy-done((s32[1,8]{1,0:T(1,128)S(1)}, s32[1,8]{1,0:T(1,128)}, u32[]{:S(2)}) %copy-start.1) | copy-done | bytes 56
  2.9 0.0 copy-start.2
  2.9 0.7 %copy-done.2 = s32[64]{0:T(128)S(1)} copy-done((s32[64]{0:T(128)S(1)}, s32[64]{0:T(128)}, u32[]{:S(2)}) %copy-start.2) | copy-done | bytes 280
  3.5 36.7 %shard_map.58 = (bf16[1024,512]{1,0:T(8,128)(2,1)S(1)}, f32[1,8]{1,0:T(1,128)S(1)}, s32[6]{0:T(128)S(1)}) custom-call(f32[1024,512]{1,0:T(8,128)S(1)} %bitcast.3, s32[1,8]{1,0:T(1,128)S(1)} %copy-done.1, s32[1,64]{1,0:T(1,128)S(1)} %bitcast.5), custom_call_target="tpu_custom_call" | custom-call | tf_op jit(solution)/shard_map/pallas_call | solution.py:332
  40.3 1.0 %copy.9 = bf16[16,64,512]{2,1,0:T(8,128)(2,1)} copy(bf16[16,64,512]{2,1,0:T(8,128)(2,1)S(1)} %bitcast.4) | data formatting | bytes 2097152
  41.3 0.5 %copy.10 = f32[1,8]{1,0:T(1,128)} copy(f32[1,8]{1,0:T(1,128)S(1)} %get-tuple-element.13) | data formatting | bytes 64
  41.8 0.5 %copy.11 = s32[6]{0:T(128)} copy(s32[6]{0:T(128)S(1)} %get-tuple-element.14) | data formatting | bytes 48
Async XLA Ops:
  0.6 1.6 %copy-start = (f32[16,64,512]{2,1,0:T(8,128)S(1)}, f32[16,64,512]{2,1,0:T(8,128)}, u32[]{:S(2)}) copy-start(f32[16,64,512]{2,1,0:T(8,128)} %param.3) | copy-start | bytes 6291460
  2.2 0.7 %copy-start.1 = (s32[1,8]{1,0:T(1,128)S(1)}, s32[1,8]{1,0:T(1,128)}, u32[]{:S(2)}) copy-start(s32[1,8]{1,0:T(1,128)} %bits.1) | copy-start | bytes 100
  2.9 0.7 %copy-start.2 = (s32[64]{0:T(128)S(1)}, s32[64]{0:T(128)}, u32[]{:S(2)}) copy-start(s32[64]{0:T(128)} %param.5) | copy-start | bytes 772

commit v2 on v1

v2 whole, which is shorter than its diff:
```python
import functools

import jax
import jax.numpy as jnp
import ml_dtypes
import numpy as np
from jax import lax
from jax.experimental import pallas as pl
from jax.experimental.pallas import tpu as pltpu
from jax.sharding import PartitionSpec as P

NZ, NXL, NY = 16, 64, 512
LANES = 128
NJ = NY // LANES
ROWS = NZ * NXL
CANDS = 64
STEPS = 6
GROUPS = 4

AL = -1.586134342
BE = -0.05298011854
GA = 0.8829110762
DE = 0.4435068522
KA = 1.149604398
QUANT_UNIT = 1.0 / 128.0
MESH = pl.DeviceIdType.MESH


def lane_iota(rows=1):
    return lax.broadcasted_iota(jnp.int32, (rows, LANES), 1)


def line_lift(get):
    memo = {}

    def state(kind, i):
        if (kind, i) not in memo:
            if kind == "d1":
                v = add(get(i), AL, get(i - 1), get(i + 1))
            elif kind == "s1":
                v = add(get(i), BE, state("d1", i - 1), state("d1", i + 1))
            elif kind == "d2":
                v = add(state("d1", i), GA, state("s1", i - 1), state("s1", i + 1))
            else:
                v = add(state("s1", i), DE, state("d2", i - 1), state("d2", i + 1))
            memo[kind, i] = v
        return memo[kind, i]

    return state


def add(v, weight, a, b):
    if v is None:
        return None
    both = a if b is None else b if a is None else a + b
    return v if both is None else v + weight * both


def crossing(get, before):
    if before:
        inner = add(get(-3), AL, get(-4), get(-2))
        return get(-1) + AL * get(-2), get(-2) + BE * inner
    return get(0), get(0) + BE * add(get(1), AL, get(0), get(2))


def edge_rows(row, keep):
    out, get = [], row
    for level in range(3):
        for before in (True, False):
            if keep(-1 if before else 0):
                out.append((level, before, crossing(get, before)))
        get = next_level(get, keep)
    return out


def next_level(get, keep):
    memo = {}

    def bounded(i):
        if not keep(i):
            return None
        if i not in memo:
            memo[i] = get(i)
        return memo[i]

    state = line_lift(bounded)
    return lambda k: KA * state("s2", 2 * k)


def edge_matrix():
    span = 64
    eye = np.eye(2 * span)

    def row(i):
        return eye[i + span] if -span <= i < span else np.zeros(2 * span)

    behind = edge_rows(row, lambda i: i < 0)
    ahead = edge_rows(row, lambda i: i >= 0)
    true = edge_rows(row, lambda i: True)
    given = np.stack([v for part in (behind, ahead) for _, _, pair in part for v in pair])
    wanted = [v for b in (True, False) for lv, side, pair in true if lv and side == b for v in pair]
    solved = np.linalg.lstsq(given.T, np.stack(wanted).T, rcond=None)[0].T
    assert np.abs(solved @ given - np.stack(wanted)).max() < 1e-9
    return solved


EDGES = edge_matrix()


def y_matrices():
    parts = []
    for level in range(3):
        s = 2**level
        m = np.eye(NY)
        sub = m[:, ::s].copy()
        for coefficient, first in ((AL, 1), (BE, 0), (GA, 1), (DE, 0)):
            sides = np.roll(sub, 1, 1) + np.roll(sub, -1, 1)
            sub[:, first::2] += coefficient * sides[:, first::2]
        sub[:, 0::2] *= KA
        sub[:, 1::2] /= KA
        m[:, ::s] = sub
        m = m[:, LANES : 3 * LANES].astype(np.float32)
        high = m.astype(ml_dtypes.bfloat16)
        low = (m - high.astype(np.float32)).astype(ml_dtypes.bfloat16)
        parts.append(np.stack([high, low]))
    return np.stack(parts)


def y_transform(buf, at, w, level):
    vals = [buf[j, at, :] for j in range(NJ)]
    high = [v.astype(jnp.bfloat16) for v in vals]
    low = [(v - h.astype(jnp.float32)).astype(jnp.bfloat16) for v, h in zip(vals, high)]
    for half in range(2):
        order = [(2 * half - 1) % NJ, 2 * half, 2 * half + 1, (2 * half + 2) % NJ]
        h = jnp.concatenate([high[o] for o in order], axis=1)
        l = jnp.concatenate([low[o] for o in order], axis=1)
        out = (
            jnp.dot(h, w[level, 0], preferred_element_type=jnp.float32)
            + jnp.dot(l, w[level, 0], preferred_element_type=jnp.float32)
            + jnp.dot(h, w[level, 1], preferred_element_type=jnp.float32)
        )
        buf[2 * half, at, :] = out[:, :LANES]
        buf[2 * half + 1, at, :] = out[:, LANES:]


def z_pass(buf, nz, nx, level):
    def z_body(i, carry):
        at = [pl.ds(pl.multiple_of(k * nx + i * 8, 8), 8) for k in range(nz)]
        for j in range(NJ):
            planes = z_lift([buf[j, at[k], :] for k in range(nz)], level)
            for k in range(nz):
                buf[j, at[k], :] = planes[k]
        return carry

    lax.fori_loop(0, nx // 8, z_body, 0)


def weights(level):
    if level == 0:
        return AL, BE, GA, DE
    own = lane_iota() % 2**level == 0
    return tuple(jnp.where(own, c, 0.0) for c in (AL, BE, GA, DE))


def z_lift(v, level):
    n = len(v)
    w = weights(level)
    v = list(v)
    for coefficient, first in ((w[0], 1), (w[1], 0), (w[2], 1), (w[3], 0)):
        for k in range(first, n, 2):
            a = v[k - 1] if k > 0 else v[k + 1]
            b = v[k + 1] if k < n - 1 else v[k - 1]
            v[k] = v[k] + coefficient * (a + b)
    return v


def shift_up(v, last):
    rows = v.shape[0]
    index = lax.broadcasted_iota(jnp.int32, v.shape, 0)
    return jnp.where(index == rows - 1, last, pltpu.roll(v, rows - 1, 0))


def shift_down(v, first):
    index = lax.broadcasted_iota(jnp.int32, v.shape, 0)
    return jnp.where(index == 0, first, pltpu.roll(v, 1, 0))


def x_lift(even, odd, p, r, e, t, level):
    rows = even.shape[0]
    al, be, ga, de = weights(level)
    d1 = odd + al * (even + shift_up(even, e))
    d1_before = p + al * even[0:1]
    s1 = even + be * (d1 + shift_down(d1, d1_before))
    s1_before = r + be * d1_before
    s1_after = t + be * d1[rows - 1 : rows]
    d2 = d1 + ga * (s1 + shift_up(s1, s1_after))
    d2_before = d1_before + ga * (s1_before + s1[0:1])
    s2 = s1 + de * (d2 + shift_down(d2, d2_before))
    return s2, d2


def kernel(
    n, x_hbm, w_hbm, bits_hbm, slopes_hbm, coded, dist, trial,
    c0, c1, c2, h0, h1, h2, w, ob, bits, slopes, slope_row, rates,
    send_right, send_left, from_left, from_right,
    in_sem, w_sem, small_sem, out_sem, rate_send, rate_recv, edge_send, edge_recv,
):
    me = lax.axis_index("gx")
    right, left = lax.rem(me + 1, n), lax.rem(me + n - 1, n)

    group_rows = ROWS // GROUPS
    loads = []
    for g in range(GROUPS):
        for j in range(NJ):
            copy = pltpu.make_async_copy(
                x_hbm.at[pl.ds(g * group_rows, group_rows), pl.ds(j * LANES, LANES)],
                c0.at[j, pl.ds(g * group_rows, group_rows)],
                in_sem.at[g, j],
            )
            copy.start()
            loads.append(copy)
    small = [
        pltpu.make_async_copy(bits_hbm, bits, small_sem.at[0]),
        pltpu.make_async_copy(slopes_hbm, slopes, small_sem.at[1]),
    ]
    w_loads = [pltpu.make_async_copy(w_hbm.at[k], w.at[k], w_sem.at[k]) for k in range(3)]
    for copy in small + w_loads:
        copy.start()

    barrier = pltpu.get_barrier_semaphore()

    def greet(k, carry):
        pl.semaphore_signal(
            barrier, inc=1, device_id={"gx": lax.rem(me + k, n)}, device_id_type=MESH
        )
        return carry

    lax.fori_loop(1, n, greet, 0)

    for copy in loads:
        copy.wait()

    def edge_body(j, carry):
        def row(i):
            return c0[j, pl.ds(i % NXL, NZ, stride=NXL), :]

        for level, _, pair in edge_rows(row, lambda i: i < 0):
            send_right[2 * level, j] = pair[0]
            send_right[2 * level + 1, j] = pair[1]
        for level, _, pair in edge_rows(row, lambda i: i >= 0):
            send_left[2 * level, j] = pair[0]
            send_left[2 * level + 1, j] = pair[1]
        return carry

    lax.fori_loop(0, NJ, edge_body, 0)

    pl.semaphore_wait(barrier, n - 1)
    copies = []
    for side, src, dst, to in (
        (0, send_right, from_left, right),
        (1, send_left, from_right, left),
    ):
        copy = pltpu.make_async_remote_copy(
            src_ref=src,
            dst_ref=dst,
            send_sem=edge_send.at[side],
            recv_sem=edge_recv.at[side],
            device_id={"gx": to},
            device_id_type=MESH,
        )
        copy.start()
        copies.append(copy)

    for copy in small:
        copy.wait()
    slope_row[...] = jnp.full((1, LANES), 536870911, jnp.int32)
    slope_row[:, 0:CANDS] = slopes[...]
    trial_slopes = slope_row[...]
    skipped = jnp.zeros((1, LANES), jnp.int32)
    for q in range(1, 16):
        skipped = skipped + jnp.where(trial_slopes > 4**q, 1, 0)
    own = jnp.zeros((1, LANES), jnp.int32)
    for b in range(8):
        own = own + jnp.maximum(bits[0, b] - skipped, 0)
    rates[me] = own

    def rate_copy(k, row):
        return pltpu.make_async_remote_copy(
            src_ref=rates.at[row],
            dst_ref=rates.at[row],
            send_sem=rate_send.at[k],
            recv_sem=rate_recv.at[k],
            device_id={"gx": lax.rem(me + k, n)},
            device_id_type=MESH,
        )

    def send_rate(k, carry):
        rate_copy(k, me).start()
        return carry

    lax.fori_loop(1, n, send_rate, 0)

    def x_pass(level, buf, nz, nx, nxt, edge, edge_nx, first):
        half = nx // 2
        step = 2**level
        own = lane_iota() % step == 0

        def x_body(i, carry):
            for parity in range(2):
                k = 2 * i + parity
                z_gain = 1.0 / KA if parity else KA
                even_scale, odd_scale = z_gain * KA, z_gain / KA
                if level:
                    even_scale = jnp.where(own, even_scale, 1.0)
                    odd_scale = jnp.where(own, odd_scale, 1.0)
                base = k * step * NXL
                for j in range(NJ):
                    even = buf[j, pl.ds(k * nx, half, stride=2), :]
                    odd = buf[j, pl.ds(k * nx + 1, half, stride=2), :]
                    p, r, e, t = [
                        edge[j, pl.ds(k * edge_nx + first + f, 1), :] for f in range(4)
                    ]
                    s2, d2 = x_lift(even, odd, p, r, e, t, level)
                    s2 = s2 * even_scale
                    d2 = d2 * odd_scale
                    c0[j, pl.ds(base + step, half, stride=2 * step), :] = d2
                    if parity == 0 and level < 2:
                        nxt[j, pl.ds(pl.multiple_of(i * half, 8), half), :] = s2
                    else:
                        c0[j, pl.ds(base, half, stride=2 * step), :] = s2
            return carry

        lax.fori_loop(0, nz // 2, x_body, 0)

    w_loads[0].wait()

    def y_body(i, carry):
        y_transform(c0, pl.ds(pl.multiple_of(i * 256, 256), 256), w, 0)
        return carry

    lax.fori_loop(0, ROWS // 256, y_body, 0)
    z_pass(c0, NZ, NXL, 0)

    for copy in copies:
        copy.wait()

    def cross_body(j, carry):
        mine_right = [send_right[f, j] for f in range(6)]
        mine_left = [send_left[f, j] for f in range(6)]
        theirs_left = [from_left[f, j] for f in range(6)]
        theirs_right = [from_right[f, j] for f in range(6)]

        def put(f, v):
            h0[j, pl.ds(f, NZ, stride=16), :] = v

        put(0, theirs_left[0])
        put(1, theirs_left[1])
        put(2, theirs_right[0])
        put(3, theirs_right[1])
        for f in range(4, 8):
            put(f, jnp.zeros((NZ, LANES), jnp.float32))
        for side, given in ((0, theirs_left + mine_left), (1, mine_right + theirs_right)):
            for f in range(4):
                total = None
                for c, v in zip(EDGES[4 * side + f], given):
                    if abs(c) > 1e-12:
                        total = float(c) * v if total is None else total + float(c) * v
                put(8 + 4 * (f // 2) + 2 * side + f % 2, total)
        return carry

    lax.fori_loop(0, NJ, cross_body, 0)
    y_transform(h0, pl.ds(0, 256), w, 0)
    z_pass(h0, NZ, 16, 0)
    x_pass(0, c0, NZ, NXL, c1, h0, 16, 0)

    w_loads[1].wait()
    for j in range(NJ):
        for k in range(NZ // 2):
            h1[j, pl.ds(8 * k, 8), :] = h0[j, pl.ds(32 * k + 8, 8), :] * KA
    y_transform(c1, pl.ds(0, 256), w, 1)
    z_pass(c1, NZ // 2, NXL // 2, 1)
    y_transform(h1, pl.ds(0, 64), w, 1)
    z_pass(h1, NZ // 2, 8, 1)
    x_pass(1, c1, NZ // 2, NXL // 2, c2, h1, 8, 0)

    w_loads[2].wait()
    for j in range(NJ):
        for k in range(NZ // 4):
            h2[j, pl.ds(8 * k, 8), :] = h1[j, pl.ds(16 * k, 8), :] * KA
    y_transform(c2, pl.ds(0, 64), w, 2)
    z_pass(c2, NZ // 4, NXL // 4, 2)
    y_transform(h2, pl.ds(0, 32), w, 2)
    z_pass(h2, NZ // 4, 8, 2)
    x_pass(2, c2, NZ // 4, NXL // 4, None, h2, 8, 4)

    def take_rate(k, carry):
        rate_copy(k, lax.rem(me - k + n, n)).wait_recv()
        return carry

    lax.fori_loop(1, n, take_rate, 0)
    total = jnp.sum(rates[...], axis=0)
    lane = lane_iota()
    target = 2 * 8 * n
    total_f = total.astype(jnp.float32)
    over = jnp.where((lane < CANDS - 1) & (total > target), 1.0, 0.0)
    lower = jnp.sum(over).astype(jnp.int32)
    for step in range(STEPS):
        span = 2 ** (STEPS - step)
        middle = (lower // span) * span + span // 2 - 1
        trial[step] = jnp.sum(jnp.where(lane == middle, total_f, 0.0)).astype(jnp.int32)
    skip = jnp.sum(jnp.where(lane == lower, skipped.astype(jnp.float32), 0.0)).astype(jnp.int32)

    step_sizes, squares = [], []
    for j in range(NJ):
        planes = jnp.where(
            lane < 64, jnp.minimum(bits[0, 2 * j], skip), jnp.minimum(bits[0, 2 * j + 1], skip)
        )
        step_sizes.append(QUANT_UNIT * jnp.left_shift(jnp.int32(1), planes).astype(jnp.float32))
        squares.append(jnp.zeros((8, LANES), jnp.float32))

    chunk = 32
    per = group_rows // chunk
    stores = []
    for g in range(GROUPS):
        def code_body(i, sums):
            at = pl.ds(pl.multiple_of(i * chunk, chunk), chunk)
            out = []
            for j in range(NJ):
                values = c0[j, at, :]
                inside = jnp.clip(values, -step_sizes[j], step_sizes[j])
                ob[at, pl.ds(j * LANES, LANES)] = (values - inside).astype(jnp.bfloat16)
                part = inside * inside
                acc = sums[j]
                for m in range(chunk // 8):
                    acc = acc + part[8 * m : 8 * m + 8]
                out.append(acc)
            return tuple(out)

        squares = lax.fori_loop(g * per, (g + 1) * per, code_body, tuple(squares))
        at = pl.ds(g * group_rows, group_rows)
        copy = pltpu.make_async_copy(ob.at[at], coded.at[at], out_sem.at[g])
        copy.start()
        stores.append(copy)

    result = jnp.zeros((1, 8), jnp.float32)
    column = lax.broadcasted_iota(jnp.int32, (1, 8), 1)
    for j in range(NJ):
        ratio = jnp.sum(squares[j], axis=0, keepdims=True) / (step_sizes[j] * step_sizes[j])
        for half in range(2):
            mine = (lane >= 64) if half else (lane < 64)
            mean = jnp.sum(jnp.where(mine, ratio, 0.0), axis=1, keepdims=True) / (NZ * 64 * 64)
            result = jnp.where(column == 2 * j + half, mean, result)
    dist[...] = result

    def end_rate(k, carry):
        rate_copy(k, me).wait_send()
        return carry

    lax.fori_loop(1, n, end_rate, 0)
    for copy in stores:
        copy.wait()


def body(snapshot, bitplanes, slopes):
    n = lax.axis_size("gx")
    vmem = pl.BlockSpec(memory_space=pltpu.VMEM)
    smem = pl.BlockSpec(memory_space=pltpu.SMEM)
    hbm = pl.BlockSpec(memory_space=pl.ANY)
    coded, dist, trial = pl.pallas_call(
        functools.partial(kernel, n),
        out_shape=(
            jax.ShapeDtypeStruct((ROWS, NY), jnp.bfloat16),
            jax.ShapeDtypeStruct((1, 8), jnp.float32),
            jax.ShapeDtypeStruct((STEPS,), jnp.int32),
        ),
        in_specs=[hbm, hbm, hbm, hbm],
        out_specs=(hbm, vmem, smem),
        scratch_shapes=[
            pltpu.VMEM((NJ, ROWS, LANES), jnp.float32),
            pltpu.VMEM((NJ, ROWS // 4, LANES), jnp.float32),
            pltpu.VMEM((NJ, ROWS // 16, LANES), jnp.float32),
            pltpu.VMEM((NJ, NZ * 16, LANES), jnp.float32),
            pltpu.VMEM((NJ, NZ // 2 * 8, LANES), jnp.float32),
            pltpu.VMEM((NJ, NZ // 4 * 8, LANES), jnp.float32),
            pltpu.VMEM((3, 2, NY, 2 * LANES), jnp.bfloat16),
            pltpu.VMEM((ROWS, NY), jnp.bfloat16),
            pltpu.SMEM((1, 8), jnp.int32),
            pltpu.VMEM((1, CANDS), jnp.int32),
            pltpu.VMEM((1, LANES), jnp.int32),
            pltpu.VMEM((n, 1, LANES), jnp.int32),
            *[pltpu.VMEM((6, NJ, NZ, LANES), jnp.float32)] * 4,
            pltpu.SemaphoreType.DMA((GROUPS, NJ)),
            pltpu.SemaphoreType.DMA((3,)),
            pltpu.SemaphoreType.DMA((2,)),
            pltpu.SemaphoreType.DMA((GROUPS,)),
            pltpu.SemaphoreType.DMA((n,)),
            pltpu.SemaphoreType.DMA((n,)),
            pltpu.SemaphoreType.DMA((2,)),
            pltpu.SemaphoreType.DMA((2,)),
        ],
        compiler_params=pltpu.CompilerParams(
            collective_id=0, has_side_effects=True, vmem_limit_bytes=60 * 1024 * 1024
        ),
    )(snapshot.reshape(ROWS, NY), jnp.asarray(y_matrices()), bitplanes, slopes.reshape(1, CANDS))
    return coded.reshape(NZ, NXL, NY), dist, trial


def solution(mesh):
    return jax.shard_map(
        body,
        mesh=mesh,
        in_specs=(P(None, ("slab", "gx"), None), P(("slab", "gx"), None), P()),
        out_specs=(P(None, ("slab", "gx"), None), P(("slab", "gx"), None), P("slab")),
        check_vma=False,
    )
```

time: 42.4 us -> 23.3 us (0.55)
  Pallas kernels: 36.7 us -> 19.2 us
  local copies, waits for them, and re-layouts: 4.89 us -> 3.32 us
    pallas_call x1, Pallas kernels: 36.7 us -> 19.2 us  [body(): pl.pallas_call(functools.partial(kernel, n), out_shape=(jax.ShapeDtypeStr...]
    unnamed x9 -> x7, local copies, waits for them, and re-layouts: 4.89 us -> 3.32 us
where the time goes in v2:
time: 23.3 us; the launch traced here: 23.1 us
  Pallas kernels  19.2 us (82%)
  local copies, waits for them, and re-layouts  3.32 us (14%)
  between operations  0.66 us (3%)
    pallas_call x1, Pallas kernels, body(): pl.pallas_call(functools.partial(kernel, n), out_shape=(jax.ShapeDtypeStr...  19.2 us
    unnamed x7, local copies, waits for them, and re-layouts  3.32 us

profile of v2, /device:TPU:0, one launch (start us, length us, event | category | flops | bytes accessed | tf_op | source)
XLA Modules:
  0.0 23.1 jit_solution(17609419654240049258)
XLA Ops:
  0.6 19.2 %shard_map.67 = (bf16[1024,512]{1,0:T(8,128)(2,1)}, f32[1,8]{1,0:T(1,128)}, s32[6]{0:T(128)}) custom-call(f32[1024,512]{1,0:T(8,128)} %bitcast.3, bf16[3,2,512,256]{3,2,1,0:T(8,128)(2,1)} %constant.2.clone.w_hbm, s32[1,8]{1,0:T(1,128)} %bits_hbm.1, s32[1,64]{1,0:T(1,128)} %bitcast.5), custom_call_target="tpu_custom_call" | custom-call | tf_op jit(solution)/shard_map/pallas_call | solution.py:469
  19.8 0.0 copy-start.1
  19.8 0.0 copy-start
  19.8 2.3 %copy.10 = bf16[16,64,512]{2,1,0:T(8,128)(2,1)} copy(bf16[16,64,512]{2,1,0:T(8,128)(2,1)} %bitcast.4) | data formatting | bytes 2097152
  22.1 0.0 copy-done.1
  22.1 0.5 %copy.11 = f32[1,8]{1,0:T(1,128)} copy(f32[1,8]{1,0:T(1,128)S(1)} %copy-done.1) | data formatting | bytes 64
  22.6 0.0 copy-done
  22.6 0.5 %copy.12 = s32[6]{0:T(128)} copy(s32[6]{0:T(128)S(1)} %copy-done) | data formatting | bytes 48
Async XLA Ops:
  19.8 2.3 %copy-start.1 = (f32[1,8]{1,0:T(1,128)S(1)}, f32[1,8]{1,0:T(1,128)}, u32[]{:S(2)}) copy-start(f32[1,8]{1,0:T(1,128)} %get-tuple-element.13) | copy-start | bytes 100
  19.8 2.8 %copy-start = (s32[6]{0:T(128)S(1)}, s32[6]{0:T(128)}, u32[]{:S(2)}) copy-start(s32[6]{0:T(128)} %get-tuple-element.14) | copy-start | bytes 76

commit v3 on v2

--- a/solution.py
+++ b/solution.py
@@ -130,22 +130,28 @@
     vals = [buf[j, at, :] for j in range(NJ)]
     high = [v.astype(jnp.bfloat16) for v in vals]
     low = [(v - h.astype(jnp.float32)).astype(jnp.bfloat16) for v, h in zip(vals, high)]
+    rows = vals[0].shape[0]
+    orders = [[(2 * half - 1 + m) % NJ for m in range(4)] for half in range(2)]
+
+    def around(parts):
+        wide = [jnp.concatenate([parts[o] for o in order], axis=1) for order in orders]
+        return jnp.concatenate(wide, axis=0)
+
+    h, l = around(high), around(low)
+    out = (
+        jnp.dot(h, w[level, 0], preferred_element_type=jnp.float32)
+        + jnp.dot(l, w[level, 0], preferred_element_type=jnp.float32)
+        + jnp.dot(h, w[level, 1], preferred_element_type=jnp.float32)
+    )
     for half in range(2):
-        order = [(2 * half - 1) % NJ, 2 * half, 2 * half + 1, (2 * half + 2) % NJ]
-        h = jnp.concatenate([high[o] for o in order], axis=1)
-        l = jnp.concatenate([low[o] for o in order], axis=1)
-        out = (
-            jnp.dot(h, w[level, 0], preferred_element_type=jnp.float32)
-            + jnp.dot(l, w[level, 0], preferred_element_type=jnp.float32)
-            + jnp.dot(h, w[level, 1], preferred_element_type=jnp.float32)
-        )
-        buf[2 * half, at, :] = out[:, :LANES]
-        buf[2 * half + 1, at, :] = out[:, LANES:]
-
-
-def z_pass(buf, nz, nx, level):
+        part = out[half * rows : (half + 1) * rows]
+        buf[2 * half, at, :] = part[:, :LANES]
+        buf[2 * half + 1, at, :] = part[:, LANES:]
+
+
+def z_pass(buf, nz, nx, level, start=0):
     def z_body(i, carry):
-        at = [pl.ds(pl.multiple_of(k * nx + i * 8, 8), 8) for k in range(nz)]
+        at = [pl.ds(pl.multiple_of(start + k * nx + i * 8, 8), 8) for k in range(nz)]
         for j in range(NJ):
             planes = z_lift([buf[j, at[k], :] for k in range(nz)], level)
             for k in range(nz):
@@ -200,10 +206,10 @@
 
 
 def kernel(
-    n, x_hbm, w_hbm, bits_hbm, slopes_hbm, coded, dist, trial,
-    c0, c1, c2, h0, h1, h2, w, ob, bits, slopes, slope_row, rates,
+    n, x_hbm, w_hbm, bits_hbm, slopes_hbm, c0, info,
+    c1, c2, h0, w, bits, slopes, slope_row, rates,
     send_right, send_left, from_left, from_right,
-    in_sem, w_sem, small_sem, out_sem, rate_send, rate_recv, edge_send, edge_recv,
+    in_sem, w_sem, small_sem, rate_send, rate_recv, edge_send, edge_recv,
 ):
     me = lax.axis_index("gx")
     right, left = lax.rem(me + 1, n), lax.rem(me + n - 1, n)
@@ -318,7 +324,7 @@
                     even = buf[j, pl.ds(k * nx, half, stride=2), :]
                     odd = buf[j, pl.ds(k * nx + 1, half, stride=2), :]
                     p, r, e, t = [
-                        edge[j, pl.ds(k * edge_nx + first + f, 1), :] for f in range(4)
+                        edge[j, pl.ds(first + k * edge_nx + f, 1), :] for f in range(4)
                     ]
                     s2, d2 = x_lift(even, odd, p, r, e, t, level)
                     s2 = s2 * even_scale
@@ -340,6 +346,31 @@
 
     lax.fori_loop(0, ROWS // 256, y_body, 0)
     z_pass(c0, NZ, NXL, 0)
+
+    def take_rate(k, carry):
+        rate_copy(k, lax.rem(me - k + n, n)).wait_recv()
+        return carry
+
+    lax.fori_loop(1, n, take_rate, 0)
+    total = jnp.sum(rates[...], axis=0)
+    lane = lane_iota()
+    target = 2 * 8 * n
+    total_f = total.astype(jnp.float32)
+    over = jnp.where((lane < CANDS - 1) & (total > target), 1.0, 0.0)
+    lower = jnp.sum(over, axis=1, keepdims=True).astype(jnp.int32)
+    found = jnp.zeros((1, LANES), jnp.float32)
+    for step in range(STEPS):
+        span = 2 ** (STEPS - step)
+        middle = (lower & (64 - span)) + (span // 2 - 1)
+        picked = jnp.sum(jnp.where(lane == middle, total_f, 0.0), axis=1, keepdims=True)
+        found = jnp.where(lane == step, picked, found)
+    skip = jnp.sum(
+        jnp.where(lane == lower, skipped.astype(jnp.float32), 0.0), axis=1, keepdims=True
+    ).astype(jnp.int32)
+    for j in range(NJ):
+        planes = jnp.minimum(jnp.where(lane < 64, bits[0, 2 * j], bits[0, 2 * j + 1]), skip)
+        info[j : j + 1] = QUANT_UNIT * jnp.left_shift(jnp.int32(1), planes).astype(jnp.float32)
+    info[4:5] = found
 
     for copy in copies:
         copy.wait()
@@ -374,52 +405,41 @@
     x_pass(0, c0, NZ, NXL, c1, h0, 16, 0)
 
     w_loads[1].wait()
+    top = ROWS // 4
     for j in range(NJ):
         for k in range(NZ // 2):
-            h1[j, pl.ds(8 * k, 8), :] = h0[j, pl.ds(32 * k + 8, 8), :] * KA
-    y_transform(c1, pl.ds(0, 256), w, 1)
+            c1[j, pl.ds(top + 8 * k, 8), :] = h0[j, pl.ds(32 * k + 8, 8), :] * KA
+    y_transform(c1, pl.ds(0, top + 64), w, 1)
     z_pass(c1, NZ // 2, NXL // 2, 1)
-    y_transform(h1, pl.ds(0, 64), w, 1)
-    z_pass(h1, NZ // 2, 8, 1)
-    x_pass(1, c1, NZ // 2, NXL // 2, c2, h1, 8, 0)
+    z_pass(c1, NZ // 2, 8, 1, top)
+    x_pass(1, c1, NZ // 2, NXL // 2, c2, c1, 8, top)
 
     w_loads[2].wait()
+    end = ROWS // 16
     for j in range(NJ):
         for k in range(NZ // 4):
-            h2[j, pl.ds(8 * k, 8), :] = h1[j, pl.ds(16 * k, 8), :] * KA
-    y_transform(c2, pl.ds(0, 64), w, 2)
+            c2[j, pl.ds(end + 8 * k, 8), :] = c1[j, pl.ds(top + 16 * k, 8), :] * KA
+    y_transform(c2, pl.ds(0, end + 32), w, 2)
     z_pass(c2, NZ // 4, NXL // 4, 2)
-    y_transform(h2, pl.ds(0, 32), w, 2)
-    z_pass(h2, NZ // 4, 8, 2)
-    x_pass(2, c2, NZ // 4, NXL // 4, None, h2, 8, 4)
-
-    def take_rate(k, carry):
-        rate_copy(k, lax.rem(me - k + n, n)).wait_recv()
-        return carry
-
-    lax.fori_loop(1, n, take_rate, 0)
-    total = jnp.sum(rates[...], axis=0)
-    lane = lane_iota()
-    target = 2 * 8 * n
-    total_f = total.astype(jnp.float32)
-    over = jnp.where((lane < CANDS - 1) & (total > target), 1.0, 0.0)
-    lower = jnp.sum(over).astype(jnp.int32)
-    for step in range(STEPS):
-        span = 2 ** (STEPS - step)
-        middle = (lower // span) * span + span // 2 - 1
-        trial[step] = jnp.sum(jnp.where(lane == middle, total_f, 0.0)).astype(jnp.int32)
-    skip = jnp.sum(jnp.where(lane == lower, skipped.astype(jnp.float32), 0.0)).astype(jnp.int32)
-
-    step_sizes, squares = [], []
-    for j in range(NJ):
-        planes = jnp.where(
-            lane < 64, jnp.minimum(bits[0, 2 * j], skip), jnp.minimum(bits[0, 2 * j + 1], skip)
-        )
-        step_sizes.append(QUANT_UNIT * jnp.left_shift(jnp.int32(1), planes).astype(jnp.float32))
-        squares.append(jnp.zeros((8, LANES), jnp.float32))
-
+    z_pass(c2, NZ // 4, 8, 2, end)
+    x_pass(2, c2, NZ // 4, NXL // 4, None, c2, 8, end + 4)
+
+    def end_rate(k, carry):
+        rate_copy(k, me).wait_send()
+        return carry
+
+    lax.fori_loop(1, n, end_rate, 0)
+
+
+def code_kernel(c0, info, coded, dist, trial, ob, out_sem):
+    group_rows = ROWS // GROUPS
     chunk = 32
     per = group_rows // chunk
+    lane = lane_iota()
+    step_sizes = [info[j : j + 1] for j in range(NJ)]
+    squares = [jnp.zeros((8, LANES), jnp.float32)] * NJ
+    for step in range(STEPS):
+        trial[step] = jnp.sum(info[4:5, step : step + 1]).astype(jnp.int32)
     stores = []
     for g in range(GROUPS):
         def code_body(i, sums):
@@ -452,11 +472,6 @@
             result = jnp.where(column == 2 * j + half, mean, result)
     dist[...] = result
 
-    def end_rate(k, carry):
-        rate_copy(k, me).wait_send()
-        return carry
-
-    lax.fori_loop(1, n, end_rate, 0)
     for copy in stores:
         copy.wait()
 
@@ -465,25 +480,24 @@
     n = lax.axis_size("gx")
     vmem = pl.BlockSpec(memory_space=pltpu.VMEM)
     smem = pl.BlockSpec(memory_space=pltpu.SMEM)
-    hbm = pl.BlockSpec(memory_space=pl.ANY)
-    coded, dist, trial = pl.pallas_call(
+    hbm = pl.BlockSpec(memory_space=pltpu.HBM)
+    snapshot = pltpu.with_memory_space_constraint(snapshot.reshape(ROWS, NY), pltpu.HBM)
+    matrices = pltpu.with_memory_space_constraint(jnp.asarray(y_matrices()), pltpu.HBM)
+    bitplanes = pltpu.with_memory_space_constraint(bitplanes, pltpu.HBM)
+    slopes = pltpu.with_memory_space_constraint(slopes.reshape(1, CANDS), pltpu.HBM)
+    coeffs, info = pl.pallas_call(
         functools.partial(kernel, n),
         out_shape=(
-            jax.ShapeDtypeStruct((ROWS, NY), jnp.bfloat16),
-            jax.ShapeDtypeStruct((1, 8), jnp.float32),
-            jax.ShapeDtypeStruct((STEPS,), jnp.int32),
+            pltpu.VMEM((NJ, ROWS, LANES), jnp.float32),
+            pltpu.VMEM((8, LANES), jnp.float32),
         ),
         in_specs=[hbm, hbm, hbm, hbm],
-        out_specs=(hbm, vmem, smem),
+        out_specs=(vmem, vmem),
         scratch_shapes=[
-            pltpu.VMEM((NJ, ROWS, LANES), jnp.float32),
-            pltpu.VMEM((NJ, ROWS // 4, LANES), jnp.float32),
-            pltpu.VMEM((NJ, ROWS // 16, LANES), jnp.float32),
+            pltpu.VMEM((NJ, ROWS // 4 + 64, LANES), jnp.float32),
+            pltpu.VMEM((NJ, ROWS // 16 + 32, LANES), jnp.float32),
             pltpu.VMEM((NJ, NZ * 16, LANES), jnp.float32),
-            pltpu.VMEM((NJ, NZ // 2 * 8, LANES), jnp.float32),
-            pltpu.VMEM((NJ, NZ // 4 * 8, LANES), jnp.float32),
             pltpu.VMEM((3, 2, NY, 2 * LANES), jnp.bfloat16),
-            pltpu.VMEM((ROWS, NY), jnp.bfloat16),
             pltpu.SMEM((1, 8), jnp.int32),
             pltpu.VMEM((1, CANDS), jnp.int32),
             pltpu.VMEM((1, LANES), jnp.int32),
@@ -492,16 +506,33 @@
             pltpu.SemaphoreType.DMA((GROUPS, NJ)),
             pltpu.SemaphoreType.DMA((3,)),
             pltpu.SemaphoreType.DMA((2,)),
-            pltpu.SemaphoreType.DMA((GROUPS,)),
             pltpu.SemaphoreType.DMA((n,)),
             pltpu.SemaphoreType.DMA((n,)),
             pltpu.SemaphoreType.DMA((2,)),
             pltpu.SemaphoreType.DMA((2,)),
         ],
         compiler_params=pltpu.CompilerParams(
-            collective_id=0, has_side_effects=True, vmem_limit_bytes=60 * 1024 * 1024
+            collective_id=0, has_side_effects=True, vmem_limit_bytes=32 * 1024 * 1024
         ),
-    )(snapshot.reshape(ROWS, NY), jnp.asarray(y_matrices()), bitplanes, slopes.reshape(1, CANDS))
+    )(snapshot, matrices, bitplanes, slopes)
+    coded, dist, trial = pl.pallas_call(
+        code_kernel,
+        out_shape=(
+            jax.ShapeDtypeStruct((ROWS, NY), jnp.bfloat16),
+            jax.ShapeDtypeStruct((1, 8), jnp.float32),
+            jax.ShapeDtypeStruct((STEPS,), jnp.int32),
+        ),
+        in_specs=[vmem, vmem],
+        out_specs=(hbm, vmem, smem),
+        scratch_shapes=[
+            pltpu.VMEM((ROWS, NY), jnp.bfloat16),
+            pltpu.SemaphoreType.DMA((GROUPS,)),
+        ],
+        compiler_params=pltpu.CompilerParams(vmem_limit_bytes=32 * 1024 * 1024),
+    )(
+        pltpu.with_memory_space_constraint(coeffs, pltpu.VMEM),
+        pltpu.with_memory_space_constraint(info, pltpu.VMEM),
+    )
     return coded.reshape(NZ, NXL, NY), dist, trial
 
 

time: 23.3 us -> 20.5 us (0.88)
  local copies, waits for them, and re-layouts: 3.32 us -> 0 us
  Pallas kernels: 19.2 us -> 19.7 us
    unnamed x7 -> x0, local copies, waits for them, and re-layouts: 3.32 us -> none
    pallas_call x1 -> x2, Pallas kernels: 19.2 us -> 19.7 us  [the longest x1 17.7 us: body(): pl.pallas_call(functools.partial(kernel, n), out_shape=(pltpu.VMEM((NJ, R...]
where the time goes in v3:
time: 20.5 us; the launch traced here: 20.3 us
  Pallas kernels  19.7 us (96%)
  between operations  0.64 us (3%)
    pallas_call x1, Pallas kernels, body(): pl.pallas_call(functools.partial(kernel, n), out_shape=(pltpu.VMEM((NJ, R...  17.7 us
    pallas_call x1, Pallas kernels, body(): pl.pallas_call(code_kernel, out_shape=(jax.ShapeDtypeStruct((ROWS, NY), j...  1.96 us

profile of v3, /device:TPU:0, one launch (start us, length us, event | category | flops | bytes accessed | tf_op | source)
XLA Modules:
  0.0 20.3 jit_solution(16250216196794604563)
XLA Ops:
  0.6 17.7 %shard_map.67 = (f32[4,1024,128]{2,1,0:T(8,128)S(1)}, f32[8,128]{1,0:T(8,128)S(1)}) custom-call(f32[1024,512]{1,0:T(8,128)} %bitcast.3, bf16[3,2,512,256]{3,2,1,0:T(8,128)(2,1)} %constant.2.clone.w_hbm, s32[1,8]{1,0:T(1,128)} %bits_hbm.1, s32[1,64]{1,0:T(1,128)} %bitcast.4), custom_call_target="tpu_custom_call" | custom-call | tf_op jit(solution)/shard_map/pallas_call | solution.py:488
  18.3 2.0 %shard_map.68 = (bf16[1024,512]{1,0:T(8,128)(2,1)}, f32[1,8]{1,0:T(1,128)}, s32[6]{0:T(128)}) custom-call(f32[4,1024,128]{2,1,0:T(8,128)S(1)} %get-tuple-element.8.c0, f32[8,128]{1,0:T(8,128)S(1)} %get-tuple-element.9.info), custom_call_target="tpu_custom_call" | custom-call | tf_op jit(solution)/shard_map/pallas_call | solution.py:518

commit v4 on v3

--- a/solution.py
+++ b/solution.py
@@ -16,6 +16,7 @@
 CANDS = 64
 STEPS = 6
 GROUPS = 4
+PARTS = 1
 
 AL = -1.586134342
 BE = -0.05298011854
@@ -158,7 +159,7 @@
                 buf[j, at[k], :] = planes[k]
         return carry
 
-    lax.fori_loop(0, nx // 8, z_body, 0)
+    lax.fori_loop(0, nx // 8, z_body, 0, unroll=True)
 
 
 def weights(level):
@@ -214,14 +215,24 @@
     me = lax.axis_index("gx")
     right, left = lax.rem(me + 1, n), lax.rem(me + n - 1, n)
 
-    group_rows = ROWS // GROUPS
+    barrier = pltpu.get_barrier_semaphore()
+
+    def greet(k, carry):
+        pl.semaphore_signal(
+            barrier, inc=1, device_id={"gx": lax.rem(me + k, n)}, device_id_type=MESH
+        )
+        return carry
+
+    lax.fori_loop(1, n, greet, 0)
+
+    group_rows = ROWS // PARTS
     loads = []
-    for g in range(GROUPS):
-        for j in range(NJ):
+    for j in range(NJ):
+        for g in range(PARTS):
             copy = pltpu.make_async_copy(
                 x_hbm.at[pl.ds(g * group_rows, group_rows), pl.ds(j * LANES, LANES)],
                 c0.at[j, pl.ds(g * group_rows, group_rows)],
-                in_sem.at[g, j],
+                in_sem.at[j, g],
             )
             copy.start()
             loads.append(copy)
@@ -233,49 +244,37 @@
     for copy in small + w_loads:
         copy.start()
 
-    barrier = pltpu.get_barrier_semaphore()
-
-    def greet(k, carry):
-        pl.semaphore_signal(
-            barrier, inc=1, device_id={"gx": lax.rem(me + k, n)}, device_id_type=MESH
-        )
-        return carry
-
-    lax.fori_loop(1, n, greet, 0)
-
-    for copy in loads:
-        copy.wait()
-
-    def edge_body(j, carry):
+
+    copies = []
+    for j in range(NJ):
+        for copy in loads[j * PARTS : (j + 1) * PARTS]:
+            copy.wait()
+
         def row(i):
             return c0[j, pl.ds(i % NXL, NZ, stride=NXL), :]
 
         for level, _, pair in edge_rows(row, lambda i: i < 0):
-            send_right[2 * level, j] = pair[0]
-            send_right[2 * level + 1, j] = pair[1]
+            send_right[j, 2 * level] = pair[0]
+            send_right[j, 2 * level + 1] = pair[1]
         for level, _, pair in edge_rows(row, lambda i: i >= 0):
-            send_left[2 * level, j] = pair[0]
-            send_left[2 * level + 1, j] = pair[1]
-        return carry
-
-    lax.fori_loop(0, NJ, edge_body, 0)
-
-    pl.semaphore_wait(barrier, n - 1)
-    copies = []
-    for side, src, dst, to in (
-        (0, send_right, from_left, right),
-        (1, send_left, from_right, left),
-    ):
-        copy = pltpu.make_async_remote_copy(
-            src_ref=src,
-            dst_ref=dst,
-            send_sem=edge_send.at[side],
-            recv_sem=edge_recv.at[side],
-            device_id={"gx": to},
-            device_id_type=MESH,
-        )
-        copy.start()
-        copies.append(copy)
+            send_left[j, 2 * level] = pair[0]
+            send_left[j, 2 * level + 1] = pair[1]
+        if j == 0:
+            pl.semaphore_wait(barrier, n - 1)
+        for side, src, dst, to in (
+            (0, send_right, from_left, right),
+            (1, send_left, from_right, left),
+        ):
+            copy = pltpu.make_async_remote_copy(
+                src_ref=src.at[j],
+                dst_ref=dst.at[j],
+                send_sem=edge_send.at[j, side],
+                recv_sem=edge_recv.at[j, side],
+                device_id={"gx": to},
+                device_id_type=MESH,
+            )
+            copy.start()
+            copies.append(copy)
 
     for copy in small:
         copy.wait()
@@ -336,7 +335,7 @@
                         c0[j, pl.ds(base, half, stride=2 * step), :] = s2
             return carry
 
-        lax.fori_loop(0, nz // 2, x_body, 0)
+        lax.fori_loop(0, nz // 2, x_body, 0, unroll=min(4, nz // 2))
 
     w_loads[0].wait()
 
@@ -372,14 +371,11 @@
         info[j : j + 1] = QUANT_UNIT * jnp.left_shift(jnp.int32(1), planes).astype(jnp.float32)
     info[4:5] = found
 
-    for copy in copies:
-        copy.wait()
-
-    def cross_body(j, carry):
-        mine_right = [send_right[f, j] for f in range(6)]
-        mine_left = [send_left[f, j] for f in range(6)]
-        theirs_left = [from_left[f, j] for f in range(6)]
-        theirs_right = [from_right[f, j] for f in range(6)]
+    def cross_rows(j):
+        mine_right = [send_right[j, f] for f in range(6)]
+        mine_left = [send_left[j, f] for f in range(6)]
+        theirs_left = [from_left[j, f] for f in range(6)]
+        theirs_right = [from_right[j, f] for f in range(6)]
 
         def put(f, v):
             h0[j, pl.ds(f, NZ, stride=16), :] = v
@@ -397,9 +393,11 @@
                     if abs(c) > 1e-12:
                         total = float(c) * v if total is None else total + float(c) * v
                 put(8 + 4 * (f // 2) + 2 * side + f % 2, total)
-        return carry
-
-    lax.fori_loop(0, NJ, cross_body, 0)
+
+    for j in range(NJ):
+        copies[2 * j].wait()
+        copies[2 * j + 1].wait()
+        cross_rows(j)
     y_transform(h0, pl.ds(0, 256), w, 0)
     z_pass(h0, NZ, 16, 0)
     x_pass(0, c0, NZ, NXL, c1, h0, 16, 0)
@@ -502,14 +500,14 @@
             pltpu.VMEM((1, CANDS), jnp.int32),
             pltpu.VMEM((1, LANES), jnp.int32),
             pltpu.VMEM((n, 1, LANES), jnp.int32),
-            *[pltpu.VMEM((6, NJ, NZ, LANES), jnp.float32)] * 4,
-            pltpu.SemaphoreType.DMA((GROUPS, NJ)),
+            *[pltpu.VMEM((NJ, 6, NZ, LANES), jnp.float32)] * 4,
+            pltpu.SemaphoreType.DMA((NJ, PARTS)),
             pltpu.SemaphoreType.DMA((3,)),
             pltpu.SemaphoreType.DMA((2,)),
             pltpu.SemaphoreType.DMA((n,)),
             pltpu.SemaphoreType.DMA((n,)),
-            pltpu.SemaphoreType.DMA((2,)),
-            pltpu.SemaphoreType.DMA((2,)),
+            pltpu.SemaphoreType.DMA((NJ, 2)),
+            pltpu.SemaphoreType.DMA((NJ, 2)),
         ],
         compiler_params=pltpu.CompilerParams(
             collective_id=0, has_side_effects=True, vmem_limit_bytes=32 * 1024 * 1024

time: 20.5 us -> 20.1 us (0.980)
  Pallas kernels: 19.7 us -> 19.3 us
    pallas_call x1, Pallas kernels: 17.7 us -> 17.3 us  [body(): pl.pallas_call(functools.partial(kernel, n), out_shape=(pltpu.VMEM((NJ, R...]
where the time goes in v4:
time: 20.1 us; the launch traced here: 19.9 us
  Pallas kernels  19.3 us (96%)
  between operations  0.64 us (3%)
    pallas_call x1, Pallas kernels, body(): pl.pallas_call(functools.partial(kernel, n), out_shape=(pltpu.VMEM((NJ, R...  17.3 us
    pallas_call x1, Pallas kernels, body(): pl.pallas_call(code_kernel, out_shape=(jax.ShapeDtypeStruct((ROWS, NY), j...  1.96 us

profile of v4, /device:TPU:0, one launch (start us, length us, event | category | flops | bytes accessed | tf_op | source)
XLA Modules:
  0.0 19.9 jit_solution(518809579028766824)
XLA Ops:
  0.6 17.3 %shard_map.67 = (f32[4,1024,128]{2,1,0:T(8,128)S(1)}, f32[8,128]{1,0:T(8,128)S(1)}) custom-call(f32[1024,512]{1,0:T(8,128)} %bitcast.3, bf16[3,2,512,256]{3,2,1,0:T(8,128)(2,1)} %constant.2.clone.w_hbm, s32[1,8]{1,0:T(1,128)} %bits_hbm.1, s32[1,64]{1,0:T(1,128)} %bitcast.4), custom_call_target="tpu_custom_call" | custom-call | tf_op jit(solution)/shard_map/pallas_call | solution.py:486
  18.0 2.0 %shard_map.68 = (bf16[1024,512]{1,0:T(8,128)(2,1)}, f32[1,8]{1,0:T(1,128)}, s32[6]{0:T(128)}) custom-call(f32[4,1024,128]{2,1,0:T(8,128)S(1)} %get-tuple-element.8.c0, f32[8,128]{1,0:T(8,128)S(1)} %get-tuple-element.9.info), custom_call_target="tpu_custom_call" | custom-call | tf_op jit(solution)/shard_map/pallas_call | solution.py:516
